TPU v7x, 32 devices: a whole 2x2x4 slice. The times are simulated.
32 devices in a mesh: groups: 2 (over x), ctx: 16 (over z, y, core).
Axes of the slice: x: 2, y: 2, z: 4, core: 2. Of those that a mesh axis runs over, the one named last changes fastest.
Arguments:
- main_queries: bfloat16 [64, 576, 4096], P(None, None, ('groups', 'ctx')), parts along dimension 2, may hold values from -48 to 48
- main_keys: bfloat16 [576, 4096], P(None, ('groups', 'ctx')), parts along dimension 1, may hold values from -6 to 6
- index_queries: bfloat16 [64, 128, 4096], P(None, None, ('groups', 'ctx')), parts along dimension 2, may hold values from -6 to 6
- index_keys: bfloat16 [128, 4096], P(None, ('groups', 'ctx')), parts along dimension 1, may hold values from -6 to 6
- head_weights: bfloat16 [64, 4096], P(None, ('groups', 'ctx')), parts along dimension 1, may hold values from -9 to 9
- block_picks: int32 [32, 4], P(('groups', 'ctx')), parts along dimension 0, may hold values from -1 to 15, as said below
Outputs:
- row_loss: float32 [4096], P(('groups', 'ctx')), parts along dimension 0
- weight_grad: float32 [64, 4096], P(None, ('groups', 'ctx')), parts along dimension 1
- key_grad: float32 [128, 4096], P(None, ('groups', 'ctx')), parts along dimension 1
There are 2 independent parts, one for each index of `groups`. A program takes and returns all parts, laid end to end along the dimension named above; each array names one. Nothing has to cross between parts.
Inputs may be any that keep to these rules, and one draw needn't show every extreme that they name: `block_picks`: row b names the key blocks of query block b: b itself first, then block 0 where b > 0, then other blocks below b; all named blocks differ, exactly min(b + 1, 4) are named, and the remaining entries are -1.
All inputs are finite; a program needn't handle non-finite values.
Results may differ from a plain program's by a relative error of at most 0.0027.
Values may be sent and summed in bfloat16 or wider, within the bound.
A program may use at most 128 MiB of HBM per device.

v0:
```python
import jax
import jax.numpy as jnp
from jax import lax
from jax.sharding import PartitionSpec as P

main_scale = 0.07216878364870322
index_scale = 0.08838834764831845
masked_value = -1e30


def group_width():
    return 8


def place_slots(picks, slot_grads, first_owner, owner_count):
    slots = slot_grads.shape[0]
    placed = jnp.zeros((owner_count,) + slot_grads.shape[1:], jnp.float32)
    for slot in range(slots):
        local = picks[slot] - first_owner
        inside = (local >= 0) & (local < owner_count) & (picks[slot] >= 0)
        spot = jnp.clip(local, 0, owner_count - 1)
        zero = jnp.zeros((), jnp.int32)
        current = lax.dynamic_index_in_dim(placed, spot, 0, keepdims=True)
        addition = jnp.where(inside, slot_grads[slot][None], 0.0)
        placed = lax.dynamic_update_slice(placed, current + addition, (spot, zero, zero))
    return placed


def shards(main_queries, main_keys, index_queries, index_keys, head_weights, block_picks):
    block = lax.axis_index("ctx")
    tokens_here = main_queries.shape[2]
    picks = block_picks[0]
    slots = picks.shape[0]
    width = slots * tokens_here
    latent_count = main_keys.shape[0]
    packed = jnp.concatenate([main_keys, index_keys], axis=0)
    channels = packed.shape[0]
    piece = lax.all_gather(packed, "ctx", axis=1, tiled=True)
    count = piece.shape[1] // tokens_here
    owners = jnp.arange(count, dtype=jnp.int32)
    onehot = (picks[:, None] == owners[None, :]).astype(jnp.bfloat16)
    moved = jnp.einsum(
        "sm,cmt->cst",
        onehot,
        piece.reshape(channels, count, tokens_here),
        preferred_element_type=jnp.float32,
    )
    selected = moved.reshape(channels, width).astype(jnp.bfloat16)
    keys_main = selected[:latent_count]
    keys_index = selected[latent_count:]
    offsets = jnp.arange(tokens_here, dtype=jnp.int32)
    row_pos = block * tokens_here + offsets
    key_pos = (picks[:, None] * tokens_here + offsets[None, :]).reshape(-1)
    valid = jnp.repeat(picks >= 0, tokens_here)
    allowed = valid[None, :] & (key_pos[None, :] <= row_pos[:, None])
    head_count = main_queries.shape[0]
    main_group = group_width()
    summed = jnp.zeros((tokens_here, width), jnp.float32)
    for first in range(0, head_count, main_group):
        scores = (
            jnp.einsum(
                "hdt,ds->hts",
                main_queries[first : first + main_group],
                keys_main,
                preferred_element_type=jnp.float32,
            )
            * main_scale
        )
        scores = jnp.where(allowed[None], scores, masked_value)
        highest = jnp.max(scores, axis=2, keepdims=True)
        powers = jnp.exp(scores - highest)
        summed = summed + jnp.sum(powers / jnp.sum(powers, axis=2, keepdims=True), axis=0)
    target = summed / head_count
    index_count = index_queries.shape[0]
    index_group = group_width()
    weights_f32 = head_weights.astype(jnp.float32)
    raw_logits = jnp.zeros((tokens_here, width), jnp.float32)
    for first in range(0, index_count, index_group):
        before = jnp.einsum(
            "jdt,ds->jts",
            index_queries[first : first + index_group],
            keys_index,
            preferred_element_type=jnp.float32,
        )
        active = jnp.maximum(before, 0.0)
        raw_logits = raw_logits + jnp.sum(
            weights_f32[first : first + index_group, :, None] * active, axis=0
        )
    logits = jnp.where(allowed, raw_logits * index_scale, masked_value)
    highest = jnp.max(logits, axis=1, keepdims=True)
    shifted = logits - highest
    powers = jnp.exp(shifted)
    denom = jnp.sum(powers, axis=1, keepdims=True)
    chosen = powers / denom
    row_loss = -jnp.sum(target * (shifted - jnp.log(denom)), axis=1)
    grad = chosen - target
    key_total = jnp.zeros((index_queries.shape[1], width), jnp.float32)
    weight_parts = []
    for first in range(0, index_count, index_group):
        group_queries = index_queries[first : first + index_group]
        before = jnp.einsum(
            "jdt,ds->jts", group_queries, keys_index, preferred_element_type=jnp.float32
        )
        active = jnp.maximum(before, 0.0)
        weight_parts.append(jnp.sum(grad[None] * active, axis=2) * index_scale)
        upstream = jnp.where(
            before > 0.0, grad[None] * weights_f32[first : first + index_group, :, None], 0.0
        ).astype(jnp.bfloat16)
        key_total = key_total + jnp.einsum(
            "jdt,jts->ds", group_queries, upstream, preferred_element_type=jnp.float32
        )
    weight_grad = jnp.concatenate(weight_parts, axis=0)
    key_total = key_total * index_scale
    feature_count = key_total.shape[0]
    slot_grads = jnp.transpose(key_total.reshape(feature_count, slots, tokens_here), (1, 0, 2))
    device_count = lax.axis_size("ctx")
    outgoing = place_slots(picks, slot_grads, 0, device_count)
    arrived = lax.all_to_all(outgoing, "ctx", split_axis=0, concat_axis=0, tiled=True)
    key_grad = jnp.sum(arrived, axis=0)
    return (row_loss, weight_grad, key_grad)


def solution(mesh):
    in_specs = (
        P(None, None, ("groups", "ctx")),
        P(None, ("groups", "ctx")),
        P(None, None, ("groups", "ctx")),
        P(None, ("groups", "ctx")),
        P(None, ("groups", "ctx")),
        P(("groups", "ctx"), None),
    )
    out_specs = (P(("groups", "ctx")), P(None, ("groups", "ctx")), P(None, ("groups", "ctx")))
    return jax.shard_map(shards, mesh=mesh, in_specs=in_specs, out_specs=out_specs, check_vma=False)
```

profile of v0, /device:TPU:0, one launch (start us, length us, event | category | flops | bytes accessed | tf_op | source)
XLA Modules:
  0.0 201.9 jit_solution(11125934113584259267)
XLA Ops:
  7.2 1.6 pad_maximum_fusion
  20.7 38.0 %all-gather.2.cloned.1.call-done = bf16[704,2048]{1,0:T(8,128)(2,1)} async-done(((bf16[704,128]{1,0:T(8,128)(2,1)}), bf16[704,2048]{1,0:T(8,128)(2,1)}) %all-gather.2.cloned.1.call-update) | async-done | bytes 2883600 | tf_op jit(solution)/shard_map/all_gather | solution.py:38
  58.8 2.7 %copy.42 = bf16[88,8,16,128]{3,2,1,0:T(8,128)(2,1)S(1)} copy(bf16[88,8,16,128]{3,1,2,0:T(8,128)(2,1)} %bitcast.301) | data formatting | bytes 5767168
  62.6 4.1 %fusion = f32[8,128,512]{1,2,0:T(8,128)} fusion(pred[128,512]{0,1:T(8,128)(4,1)S(1)} %compare_and_fusion, bf16[576,512,1]{1,0,2:T(8,128)(2,1)S(1)} %reshape.276, bf16[64,576,128]{2,1,0:T(8,128)(2,1)} %param.6), kind=kOutput, calls=%fused_computation | convolution fusion | flops 605555712 | bytes 3932160 | tf_op jit(solution)/shard_map/div | solution.py:72
  66.7 4.0 %fusion.2 = f32[8,128,512]{1,2,0:T(8,128)} fusion(pred[128,512]{0,1:T(8,128)(4,1)S(1)} %compare_and_fusion, bf16[576,512,1]{1,0,2:T(8,128)(2,1)S(1)} %reshape.276, bf16[64,576,128]{2,1,0:T(8,128)(2,1)} %param.6), kind=kOutput, calls=%fused_computation.2 | convolution fusion | flops 605555712 | bytes 3932160 | tf_op jit(solution)/shard_map/div | solution.py:72
  70.8 4.1 %fusion.4 = f32[8,128,512]{1,2,0:T(8,128)} fusion(pred[128,512]{0,1:T(8,128)(4,1)S(1)} %compare_and_fusion, bf16[576,512,1]{1,0,2:T(8,128)(2,1)S(1)} %reshape.276, bf16[64,576,128]{2,1,0:T(8,128)(2,1)} %param.6), kind=kOutput, calls=%fused_computation.4 | convolution fusion | flops 605555712 | bytes 3932160 | tf_op jit(solution)/shard_map/div | solution.py:72
  74.9 4.1 %fusion.6 = f32[8,128,512]{1,2,0:T(8,128)} fusion(pred[128,512]{0,1:T(8,128)(4,1)S(1)} %compare_and_fusion, bf16[576,512,1]{1,0,2:T(8,128)(2,1)S(1)} %reshape.276, bf16[64,576,128]{2,1,0:T(8,128)(2,1)} %param.6), kind=kOutput, calls=%fused_computation.6 | convolution fusion | flops 605555712 | bytes 3932160 | tf_op jit(solution)/shard_map/div | solution.py:72
  79.0 4.1 %fusion.8 = f32[8,128,512]{1,2,0:T(8,128)} fusion(pred[128,512]{0,1:T(8,128)(4,1)S(1)} %compare_and_fusion, bf16[576,512,1]{1,0,2:T(8,128)(2,1)S(1)} %reshape.276, bf16[64,576,128]{2,1,0:T(8,128)(2,1)} %param.6), kind=kOutput, calls=%fused_computation.8 | convolution fusion | flops 605555712 | bytes 3932160 | tf_op jit(solution)/shard_map/div | solution.py:72
  83.1 4.0 %fusion.10 = f32[8,128,512]{1,2,0:T(8,128)} fusion(pred[128,512]{0,1:T(8,128)(4,1)S(1)} %compare_and_fusion, bf16[576,512,1]{1,0,2:T(8,128)(2,1)S(1)} %reshape.276, bf16[64,576,128]{2,1,0:T(8,128)(2,1)} %param.6), kind=kOutput, calls=%fused_computation.10 | convolution fusion | flops 605555712 | bytes 3932160 | tf_op jit(solution)/shard_map/div | solution.py:72
  87.1 4.1 %fusion.12 = f32[8,128,512]{1,2,0:T(8,128)} fusion(pred[128,512]{0,1:T(8,128)(4,1)S(1)} %compare_and_fusion, bf16[576,512,1]{1,0,2:T(8,128)(2,1)S(1)} %reshape.276, bf16[64,576,128]{2,1,0:T(8,128)(2,1)} %param.6), kind=kOutput, calls=%fused_computation.12 | convolution fusion | flops 605555712 | bytes 3932160 | tf_op jit(solution)/shard_map/div | solution.py:72
  91.2 4.2 %fusion.14 = f32[8,128,512]{1,2,0:T(8,128)} fusion(pred[128,512]{0,1:T(8,128)(4,1)S(1)} %compare_and_fusion, bf16[576,512,1]{1,0,2:T(8,128)(2,1)S(1)} %reshape.276, bf16[64,576,128]{2,1,0:T(8,128)(2,1)} %param.6), kind=kOutput, calls=%fused_computation.14 | convolution fusion | flops 605555712 | bytes 3932160 | tf_op jit(solution)/shard_map/div | solution.py:72
  95.5 1.8 fusion.16
  97.3 2.5 %fusion.18 = (f32[128,512]{0,1:T(8,128)}, f32[512,8,128]{2,0,1:T(8,128)}) fusion(f32[8,128]{1,0:T(8,128)S(1)} %get-tuple-element.24, bf16[64,128,128]{2,1,0:T(8,128)(2,1)S(1)} %copy-done.7, bf16[16,8,4,128]{3,2,1,0:T(4,128)(2,1)S(1)} %bitcast.294), kind=kOutput, calls=%fused_computation.22 | convolution fusion | flops 135725056 | bytes 2756608 | tf_op jit(solution)/shard_map/jdt,ds->jts/dot_general | solution.py:79
  99.8 2.7 %fusion.20 = (f32[128,512]{0,1:T(8,128)}, f32[512,8,128]{2,0,1:T(8,128)}) fusion(f32[8,128]{1,0:T(8,128)S(1)} %get-tuple-element.23, bf16[64,128,128]{2,1,0:T(8,128)(2,1)S(1)} %copy-done.7, bf16[16,8,4,128]{3,2,1,0:T(4,128)(2,1)S(1)} %bitcast.295), kind=kOutput, calls=%fused_computation.26 | convolution fusion | flops 135725056 | bytes 2756608 | tf_op jit(solution)/shard_map/jdt,ds->jts/dot_general | solution.py:79
  102.5 2.5 %fusion.22 = (f32[128,512]{0,1:T(8,128)}, f32[512,8,128]{2,0,1:T(8,128)}) fusion(f32[8,128]{1,0:T(8,128)S(1)} %get-tuple-element.22, bf16[64,128,128]{2,1,0:T(8,128)(2,1)S(1)} %copy-done.7, bf16[16,8,4,128]{3,2,1,0:T(4,128)(2,1)S(1)} %bitcast.296), kind=kOutput, calls=%fused_computation.30 | convolution fusion | flops 135725056 | bytes 2756608 | tf_op jit(solution)/shard_map/jdt,ds->jts/dot_general | solution.py:79
  105.0 2.6 %fusion.24 = (f32[128,512]{0,1:T(8,128)}, f32[512,8,128]{2,0,1:T(8,128)}) fusion(f32[8,128]{1,0:T(8,128)S(1)} %get-tuple-element.21, bf16[64,128,128]{2,1,0:T(8,128)(2,1)S(1)} %copy-done.7, bf16[16,8,4,128]{3,2,1,0:T(4,128)(2,1)S(1)} %bitcast.297), kind=kOutput, calls=%fused_computation.34 | convolution fusion | flops 135725056 | bytes 2756608 | tf_op jit(solution)/shard_map/jdt,ds->jts/dot_general | solution.py:79
  107.5 2.5 %fusion.26 = (f32[128,512]{0,1:T(8,128)}, f32[512,8,128]{2,0,1:T(8,128)}) fusion(f32[8,128]{1,0:T(8,128)S(1)} %get-tuple-element.20, bf16[64,128,128]{2,1,0:T(8,128)(2,1)S(1)} %copy-done.7, bf16[16,8,4,128]{3,2,1,0:T(4,128)(2,1)S(1)} %bitcast.298), kind=kOutput, calls=%fused_computation.38 | convolution fusion | flops 135725056 | bytes 2756608 | tf_op jit(solution)/shard_map/jdt,ds->jts/dot_general | solution.py:79
  110.0 2.1 %fusion.30 = (f32[128,512]{0,1:T(8,128)}, f32[512,8,128]{2,0,1:T(8,128)S(1)}) fusion(f32[8,128]{1,0:T(8,128)S(1)} %get-tuple-element.19, bf16[64,128,128]{2,1,0:T(8,128)(2,1)} %param.8, bf16[16,8,4,128]{3,2,1,0:T(4,128)(2,1)S(1)} %bitcast.299), kind=kOutput, calls=%fused_computation.46 | convolution fusion | flops 135725056 | bytes 2756608 | tf_op jit(solution)/shard_map/jdt,ds->jts/dot_general | solution.py:79
  112.2 3.5 %fusion.28 = (f32[128,512]{0,1:T(8,128)}, f32[512,8,128]{2,0,1:T(8,128)}) fusion(f32[8,128]{1,0:T(8,128)S(1)} %get-tuple-element.18, bf16[64,128,128]{2,1,0:T(8,128)(2,1)} %param.8, bf16[16,8,4,128]{3,2,1,0:T(4,128)(2,1)S(1)} %bitcast.300), kind=kOutput, calls=%fused_computation.42 | convolution fusion | flops 135725056 | bytes 2756608 | tf_op jit(solution)/shard_map/jdt,ds->jts/dot_general | solution.py:79
  115.6 4.3 %divide_reduce_fusion = f32[128,512]{0,1:T(8,128)} fusion(f32[8,128,512]{1,2,0:T(8,128)} %fusion, pred[128,512]{0,1:T(8,128)(4,1)S(1)} %compare_and_fusion, bf16[576,512,1]{1,0,2:T(8,128)(2,1)S(1)} %reshape.276, bf16[64,576,128]{2,1,0:T(8,128)(2,1)} %param.6), kind=kOutput, calls=%fused_computation.72 | convolution fusion | flops 606537216 | bytes 4194304 | tf_op jit(solution)/shard_map/sub | solution.py:71
  119.9 4.3 %divide_reduce_fusion.1 = f32[128,512]{0,1:T(8,128)} fusion(f32[8,128,512]{1,2,0:T(8,128)} %fusion.2, pred[128,512]{0,1:T(8,128)(4,1)S(1)} %compare_and_fusion, bf16[576,512,1]{1,0,2:T(8,128)(2,1)S(1)} %reshape.276, bf16[64,576,128]{2,1,0:T(8,128)(2,1)} %param.6), kind=kOutput, calls=%fused_computation.73 | convolution fusion | flops 606537216 | bytes 4194304 | tf_op jit(solution)/shard_map/sub | solution.py:71
  124.2 4.3 %divide_reduce_fusion.2 = f32[128,512]{0,1:T(8,128)} fusion(f32[8,128,512]{1,2,0:T(8,128)} %fusion.4, pred[128,512]{0,1:T(8,128)(4,1)S(1)} %compare_and_fusion, bf16[576,512,1]{1,0,2:T(8,128)(2,1)S(1)} %reshape.276, bf16[64,576,128]{2,1,0:T(8,128)(2,1)} %param.6), kind=kOutput, calls=%fused_computation.74 | convolution fusion | flops 606537216 | bytes 4194304 | tf_op jit(solution)/shard_map/sub | solution.py:71
  128.4 4.3 %divide_reduce_fusion.3 = f32[128,512]{0,1:T(8,128)} fusion(f32[8,128,512]{1,2,0:T(8,128)} %fusion.6, pred[128,512]{0,1:T(8,128)(4,1)S(1)} %compare_and_fusion, bf16[576,512,1]{1,0,2:T(8,128)(2,1)S(1)} %reshape.276, bf16[64,576,128]{2,1,0:T(8,128)(2,1)} %param.6), kind=kOutput, calls=%fused_computation.75 | convolution fusion | flops 606537216 | bytes 4194304 | tf_op jit(solution)/shard_map/sub | solution.py:71
  132.7 4.3 %divide_reduce_fusion.4 = f32[128,512]{0,1:T(8,128)} fusion(f32[8,128,512]{1,2,0:T(8,128)} %fusion.8, pred[128,512]{0,1:T(8,128)(4,1)S(1)} %compare_and_fusion, bf16[576,512,1]{1,0,2:T(8,128)(2,1)S(1)} %reshape.276, bf16[64,576,128]{2,1,0:T(8,128)(2,1)} %param.6), kind=kOutput, calls=%fused_computation.76 | convolution fusion | flops 606537216 | bytes 4194304 | tf_op jit(solution)/shard_map/sub | solution.py:71
  137.0 4.3 %divide_reduce_fusion.5 = f32[128,512]{0,1:T(8,128)} fusion(f32[8,128,512]{1,2,0:T(8,128)} %fusion.10, pred[128,512]{0,1:T(8,128)(4,1)S(1)} %compare_and_fusion, bf16[576,512,1]{1,0,2:T(8,128)(2,1)S(1)} %reshape.276, bf16[64,576,128]{2,1,0:T(8,128)(2,1)} %param.6), kind=kOutput, calls=%fused_computation.77 | convolution fusion | flops 606537216 | bytes 4194304 | tf_op jit(solution)/shard_map/sub | solution.py:71
  141.2 4.2 %divide_reduce_fusion.6 = f32[128,512]{0,1:T(8,128)} fusion(f32[8,128,512]{1,2,0:T(8,128)} %fusion.12, pred[128,512]{0,1:T(8,128)(4,1)S(1)} %compare_and_fusion, bf16[576,512,1]{1,0,2:T(8,128)(2,1)S(1)} %reshape.276, bf16[64,576,128]{2,1,0:T(8,128)(2,1)} %param.6), kind=kOutput, calls=%fused_computation.78 | convolution fusion | flops 606537216 | bytes 4194304 | tf_op jit(solution)/shard_map/sub | solution.py:71
  145.5 4.5 %divide_reduce_fusion.7 = f32[128,512]{0,1:T(8,128)} fusion(f32[8,128,512]{1,2,0:T(8,128)} %fusion.14, pred[128,512]{0,1:T(8,128)(4,1)S(1)} %compare_and_fusion, bf16[576,512,1]{1,0,2:T(8,128)(2,1)S(1)} %reshape.276, bf16[64,576,128]{2,1,0:T(8,128)(2,1)} %param.6), kind=kOutput, calls=%fused_computation.79 | convolution fusion | flops 606537216 | bytes 4194304 | tf_op jit(solution)/shard_map/sub | solution.py:71
  150.0 1.8 fusion.227
  151.9 2.0 %divide_subtract_fusion = (f32[128,512]{0,1:T(8,128)S(1)}, f32[128,512]{0,1:T(8,128)}) fusion(f32[128,512]{0,1:T(8,128)S(1)} %get-tuple-element.17, f32[128]{0:T(128)S(1)} %exponential_reduce_fusion, f32[128]{0:T(128)S(1)} %get-tuple-element.16, f32[128,512]{0,1:T(8,128)S(1)} %copy-done.11, f32[128,512]{0,1:T(8,128)S(1)} %copy-done.12, ...), kind=kLoop, calls=%fused_computation.178 | loop fusion | flops 720896 | bytes 2884608 | tf_op jit(solution)/shard_map/sub | solution.py:96
  167.7 3.7 %all-to-all-start = ((f32[16,128,128]{1,2,0:T(8,128)}), f32[16,128,128]{1,2,0:T(8,128)S(1)}, u32[]{:S(2)}, u32[]{:S(2)}) async-start(f32[16,128,128]{1,2,0:T(8,128)} %fusion.146), calls=%async_computation | async-start | bytes 2097152 | tf_op jit(solution)/shard_map/all_to_all | solution.py:118
  171.4 6.6 %fusion.17 = (f32[8,128]{1,0:T(8,128)S(1)}, f32[8,128]{1,0:T(8,128)S(1)}, f32[8,128]{1,0:T(8,128)S(1)}, f32[8,128]{1,0:T(8,128)S(1)}, f32[8,128]{1,0:T(8,128)S(1...) fusion(f32[512,8,128]{2,0,1:T(8,128)} %get-tuple-element.31, f32[128,512]{0,1:T(8,128)} %copy-done.9, ...), kind=kLoop, calls=%fused_computation.19 | loop fusion | flops 12574720 | bytes 17072128 | tf_op jit(solution)/shard_map/reduce_sum | solution.py:105
  178.8 15.5 %all-to-all-done = f32[16,128,128]{1,2,0:T(8,128)S(1)} async-done(((f32[16,128,128]{1,2,0:T(8,128)}), f32[16,128,128]{1,2,0:T(8,128)S(1)}, u32[]{:S(2)}, u32[]{:S(2)}) %all-to-all-start) | async-done | bytes 1048608 | tf_op jit(solution)/shard_map/all_to_all | solution.py:118
  (77 shorter events, 20.3 us)
Async XLA Ops:
  7.2 51.6 %all-gather.2.cloned.1.call-start = ((), (), s32[]{:S(2)}) async-start(), calls=%async_computation.1 | async-start | bytes 3063808 | tf_op jit(solution)/shard_map/all_gather | solution.py:38
  58.8 2.7 %copy-start.16 = (s32[1,4]{1,0:T(1,128)S(1)}, s32[1,4]{1,0:T(1,128)}, u32[]{:S(2)}) copy-start(s32[1,4]{1,0:T(1,128)} %param.11) | copy-start | bytes 52
  91.2 4.2 %copy-start.7 = (bf16[64,128,128]{2,1,0:T(8,128)(2,1)S(1)}, bf16[64,128,128]{2,1,0:T(8,128)(2,1)}, u32[]{:S(2)}) copy-start(bf16[64,128,128]{2,1,0:T(8,128)(2,1)} %param.8) | copy-start | bytes 6291460
  149.9 1.9 copy-start.11
  149.9 1.9 copy-start.12
  149.9 1.9 copy-start.13
  149.9 1.9 copy-start.14
  149.9 1.9 copy-start.15
  149.9 4.0 %copy-start.8 = (bf16[64,128,128]{2,1,0:T(8,128)(2,1)S(1)}, bf16[64,128,128]{2,1,0:T(8,128)(2,1)}, u32[]{:S(2)}) copy-start(bf16[64,128,128]{2,1,0:T(8,128)(2,1)} %param.8) | copy-start | bytes 6291460
  151.8 2.2 %copy-start.6 = (f32[512,8,128]{2,0,1:T(8,128)S(1)}, f32[512,8,128]{2,0,1:T(8,128)}, u32[]{:S(2)}) copy-start(f32[512,8,128]{2,0,1:T(8,128)} %get-tuple-element.45) | copy-start | bytes 6291460
  153.9 7.2 %copy-start.9 = (f32[128,512]{0,1:T(8,128)}, f32[128,512]{0,1:T(8,128)S(1)}, u32[]{:S(2)}) copy-start(f32[128,512]{0,1:T(8,128)S(1)} %get-tuple-element.14) | copy-start | bytes 786436
  153.9 1.7 copy-start.5
  154.4 2.0 copy-start.4
  156.1 1.7 copy-start.3
  156.8 1.7 copy-start.2
  158.2 1.7 copy-start.1
  159.0 1.7 copy-start
  167.7 26.6 %all-to-all-start = ((f32[16,128,128]{1,2,0:T(8,128)}), f32[16,128,128]{1,2,0:T(8,128)S(1)}, u32[]{:S(2)}, u32[]{:S(2)}) async-start(f32[16,128,128]{1,2,0:T(8,128)} %fusion.146), calls=%async_computation | async-start | bytes 2097152 | tf_op jit(solution)/shard_map/all_to_all | solution.py:118
  171.4 6.7 %copy-start.10 = (f32[128,512]{0,1:T(8,128)S(1)}, f32[128,512]{0,1:T(8,128)}, u32[]{:S(2)}) copy-start(f32[128,512]{0,1:T(8,128)} %get-tuple-element.15) | copy-start | bytes 786436
  178.8 16.3 %copy-start.17 = (f32[64,128]{1,0:T(8,128)}, f32[64,128]{1,0:T(8,128)S(1)}, u32[]{:S(2)}) copy-start(f32[64,128]{1,0:T(8,128)S(1)} %constant_dynamic-update-slice_fusion) | copy-start | bytes 98308
Sparse Core Ops, SparseCore 0:
  10.2 48.5 all-gather.1
where the time goes:
time: 204 us; the launch traced here: 202 us
  matrix products  91.4 us (45%)
  waiting for transfers between devices  53.6 us (26%)
  between operations  22.3 us (11%)
  other arithmetic  19.5 us (10%)
  local copies, waits for them, and re-layouts  11.5 us (6%)
  starting transfers between devices  3.69 us (2%)
    all_gather x1, waiting for transfers between devices, shards(): piece = lax.all_gather(packed, 'ctx', axis=1, tiled=True)  38 us
    sub x8, matrix products, shards(): powers = jnp.exp(scores - highest)  34.3 us
    div x8, matrix products, shards(): powers / jnp.sum(powers, axis=2, keepdims=True)  32.9 us
    dot_general x8, matrix products, shards(): jnp.einsum('jdt,ds->jts', index_queries[first:first + index_group], keys_...  20.2 us
    all_to_all x1, waiting for transfers between devices, shards(): lax.all_to_all(outgoing, 'ctx', split_axis=0, concat_axis=0, tiled=True)  15.5 us
    unnamed x38, local copies, waits for them, and re-layouts  7.58 us
    reduce_sum x1, other arithmetic, shards(): weight_parts.append(jnp.sum(grad[None] * active, axis=2) * index_scale)  6.64 us
    dynamic_update_slice x4, other arithmetic, place_slots(): lax.dynamic_update_slice(placed, current + addition, (spot, zero, zero))  5.02 us
  transfers between devices with their start and end apart: 2, of which 2 were waited for; matrix products, arithmetic and copies ran while one was open for 6% of the time, Pallas kernels for 0%

commit v1 on v0

v1 whole, which is shorter than its diff:
```python
import functools

import jax
import jax.numpy as jnp
from jax import lax
from jax.experimental import pallas as pl
from jax.experimental.pallas import tpu as pltpu
from jax.sharding import PartitionSpec as P

main_scale = 0.07216878364870322
index_scale = 0.08838834764831845
masked_value = -1e30
log2e = 1.4426950408889634


def compute_kernel(
    picks, mq, iq, hw, k0, k1, k2, k3, loss_ref, wg_ref, slot_ref, km, ki, eye, acc, raw, kt, gr, wf
):
    step = pl.program_id(0)
    steps = pl.num_programs(0)
    tok = mq.shape[2]
    latent = mq.shape[1]
    heads = mq.shape[0]
    slots = 4
    width = slots * tok

    @pl.when(step == 0)
    def _():
        rows = lax.broadcasted_iota(jnp.int32, (tok, tok), 0)
        cols = lax.broadcasted_iota(jnp.int32, (tok, tok), 1)
        diag = jnp.where(rows == cols, 1.0, 0.0).astype(jnp.bfloat16)
        eye[:, :tok] = diag
        eye[:, tok:] = diag
        for slot, key in enumerate((k0, k1, k2, k3)):
            here = pl.ds(slot * tok, tok)
            km[here, :latent] = key[0, :latent, :].T
            ki[here, :] = key[0, latent:, :].T
            if slot == 0:
                bias = jnp.where(rows > cols, masked_value, 0.0)
            else:
                bias = jnp.full((tok, tok), jnp.where(picks[0, slot] >= 0, 0.0, masked_value))
            km[here, latent:] = bias.astype(jnp.bfloat16)
        wf[...] = hw[...].astype(jnp.float32)
        acc[...] = jnp.zeros_like(acc)
        raw[...] = jnp.zeros_like(raw)

    scale2 = main_scale * log2e

    def main_pair(i, _):
        h = 2 * i
        pair = jnp.concatenate([mq[h], mq[h + 1]], axis=1)
        query = jnp.concatenate([pair, eye[...]], axis=0)
        s = jnp.dot(km[...], query, preferred_element_type=jnp.float32)
        m = jnp.max(s, axis=0, keepdims=True)
        p = jnp.exp2((s - m) * scale2)
        p = p * (1.0 / jnp.sum(p, axis=0, keepdims=True))
        acc[...] += p[:, :tok] + p[:, tok:]
        j = step * heads + h
        ipair = jnp.concatenate([iq[j], iq[j + 1]], axis=1)
        before = jnp.dot(ki[...], ipair, preferred_element_type=jnp.float32)
        w = jnp.concatenate(
            [wf[pl.ds(j, 1), :], wf[pl.ds(j + 1, 1), :]], axis=1
        )
        a = jnp.maximum(before, 0.0) * w
        raw[...] += a[:, :tok] + a[:, tok:]
        return 0

    lax.fori_loop(0, heads // 2, main_pair, 0, unroll=2)

    @pl.when(step == steps - 1)
    def _():
        total_heads = heads * steps
        index_heads = iq.shape[0]
        target = acc[...] * (1.0 / total_heads)
        bias = km[:, latent:].astype(jnp.float32)
        logits = jnp.where(bias < 0.0, masked_value, raw[...] * index_scale)
        highest = jnp.max(logits, axis=0, keepdims=True)
        shifted = logits - highest
        powers = jnp.exp(shifted)
        denom = jnp.sum(powers, axis=0, keepdims=True)
        loss_ref[...] = -jnp.sum(target * (shifted - jnp.log(denom)), axis=0, keepdims=True)
        grad = powers / denom - target
        gr[:, :tok] = grad
        gr[:, tok:] = grad
        kt[...] = jnp.zeros_like(kt)

        def back_pair(i, _):
            j = 2 * i
            ipair = jnp.concatenate([iq[j], iq[j + 1]], axis=1)
            before = jnp.dot(ki[...], ipair, preferred_element_type=jnp.float32)
            g = gr[...]
            w = jnp.concatenate(
                [wf[pl.ds(j, 1), :], wf[pl.ds(j + 1, 1), :]], axis=1
            )
            part = jnp.sum(g * jnp.maximum(before, 0.0), axis=0, keepdims=True) * index_scale
            wg_ref[pl.ds(j, 1), :] = part[:, :tok]
            wg_ref[pl.ds(j + 1, 1), :] = part[:, tok:]
            up = jnp.where(before > 0.0, g * w, 0.0).astype(jnp.bfloat16)
            kt[...] += lax.dot_general(
                up, ipair, (((1,), (1,)), ((), ())), preferred_element_type=jnp.float32
            )
            return 0

        lax.fori_loop(0, index_heads // 2, back_pair, 0, unroll=2)
        for slot in range(slots):
            slot_ref[slot] = (kt[pl.ds(slot * tok, tok), :] * index_scale).T


def compute(picks, mq, iq, hw, keys):
    heads, latent, tok = mq.shape
    index_heads, dim, _ = iq.shape
    channels = latent + dim
    group = 8
    width = 4 * tok

    def key_spec(slot):
        return pl.BlockSpec(
            (1, channels, tok), lambda g, p: (jnp.maximum(p[0, slot], 0), 0, 0)
        )

    spec = pltpu.PrefetchScalarGridSpec(
        num_scalar_prefetch=1,
        grid=(heads // group,),
        in_specs=[
            pl.BlockSpec((group, latent, tok), lambda g, p: (g, 0, 0)),
            pl.BlockSpec((index_heads, dim, tok), lambda g, p: (0, 0, 0)),
            pl.BlockSpec((index_heads, tok), lambda g, p: (0, 0)),
        ]
        + [key_spec(slot) for slot in range(4)],
        out_specs=[
            pl.BlockSpec((1, tok), lambda g, p: (0, 0)),
            pl.BlockSpec((index_heads, tok), lambda g, p: (0, 0)),
            pl.BlockSpec((4, dim, tok), lambda g, p: (0, 0, 0)),
        ],
        scratch_shapes=[
            pltpu.VMEM((width, latent + tok), jnp.bfloat16),
            pltpu.VMEM((width, dim), jnp.bfloat16),
            pltpu.VMEM((tok, 2 * tok), jnp.bfloat16),
            pltpu.VMEM((width, tok), jnp.float32),
            pltpu.VMEM((width, tok), jnp.float32),
            pltpu.VMEM((width, dim), jnp.float32),
            pltpu.VMEM((width, 2 * tok), jnp.float32),
            pltpu.VMEM((index_heads, tok), jnp.float32),
        ],
    )
    return pl.pallas_call(
        compute_kernel,
        grid_spec=spec,
        out_shape=[
            jax.ShapeDtypeStruct((1, tok), jnp.float32),
            jax.ShapeDtypeStruct((index_heads, tok), jnp.float32),
            jax.ShapeDtypeStruct((4, dim, tok), jnp.float32),
        ],
        compiler_params=pltpu.CompilerParams(vmem_limit_bytes=48 * 1024 * 1024),
    )(picks, mq, iq, hw, keys, keys, keys, keys)


def shards(main_queries, main_keys, index_queries, index_keys, head_weights, block_picks):
    tok = main_queries.shape[2]
    picks = block_picks
    count = lax.axis_size("ctx")
    packed = jnp.concatenate([main_keys, index_keys], axis=0)
    keys = lax.all_gather(packed, "ctx", axis=0, tiled=False)
    row_loss, weight_grad, slot_grads = compute(
        picks, main_queries, index_queries, head_weights, keys
    )
    owners = jnp.arange(count, dtype=jnp.int32)
    match = picks[0][:, None] == owners[None, :]
    outgoing = jnp.zeros((count,) + slot_grads.shape[1:], jnp.float32)
    for slot in range(4):
        outgoing = outgoing + jnp.where(match[slot][:, None, None], slot_grads[slot][None], 0.0)
    arrived = lax.all_to_all(outgoing, "ctx", split_axis=0, concat_axis=0, tiled=True)
    key_grad = jnp.sum(arrived, axis=0)
    return (row_loss.reshape(tok), weight_grad, key_grad)


def solution(mesh):
    in_specs = (
        P(None, None, ("groups", "ctx")),
        P(None, ("groups", "ctx")),
        P(None, None, ("groups", "ctx")),
        P(None, ("groups", "ctx")),
        P(None, ("groups", "ctx")),
        P(("groups", "ctx"), None),
    )
    out_specs = (P(("groups", "ctx")), P(None, ("groups", "ctx")), P(None, ("groups", "ctx")))
    return jax.shard_map(shards, mesh=mesh, in_specs=in_specs, out_specs=out_specs, check_vma=False)
```

time: 204 us -> 126 us (0.62)
  matrix products: 91.4 us -> 0 us
  Pallas kernels: 0 us -> 27.9 us
  blocking collectives: 0 us -> 27.7 us
  other arithmetic: 19.5 us -> 3.41 us
  between operations: 22.3 us -> 14 us
  local copies, waits for them, and re-layouts: 11.5 us -> 4.81 us
  waiting for transfers between devices: 53.6 us -> 47.8 us
  starting transfers between devices: 3.69 us -> 0.04 us
    sub x8 -> x0, matrix products: 34.3 us -> none  [shards(): powers = jnp.exp(scores - highest)]
    div x8 -> x0, matrix products: 32.9 us -> none  [shards(): powers / jnp.sum(powers, axis=2, keepdims=True)]
    pallas_call x0 -> x1, Pallas kernels: none -> 27.9 us  [compute(): pl.pallas_call(compute_kernel, grid_spec=spec, out_shape=[jax.ShapeDtypeS...]
    all_to_all x0 -> x1, blocking collectives: none -> 27.7 us  [shards(): lax.all_to_all(outgoing, 'ctx', split_axis=0, concat_axis=0, tiled=True)]
    dot_general x17 -> x0, matrix products: 24.2 us -> none  [the longest x8 20.2 us: shards(): jnp.einsum('jdt,ds->jts', index_queries[first:first + index_group], keys_...]
    all_to_all x1 -> x0, waiting for transfers between devices: 15.5 us -> none  [shards(): lax.all_to_all(outgoing, 'ctx', split_axis=0, concat_axis=0, tiled=True)]
    all_gather x1, waiting for transfers between devices: 38 us -> 47.8 us  [shards(): keys = lax.all_gather(packed, 'ctx', axis=0, tiled=False)]
    reduce_sum x3 -> x0, other arithmetic: 6.82 us -> none  [the longest x1 6.64 us: shards(): weight_parts.append(jnp.sum(grad[None] * active, axis=2) * index_scale)]
  transfers between devices with their start and end apart: 2 -> 1, of which waited for: 2 -> 1; matrix products, arithmetic and copies ran while one was open for 6% -> 1% of each run, Pallas kernels for 0% -> 0%
where the time goes in v1:
time: 126 us
  waiting for transfers between devices  47.8 us (38%)
  Pallas kernels  27.9 us (22%)
  blocking collectives  27.7 us (22%)
  between operations  14 us (11%)
  local copies, waits for them, and re-layouts  4.81 us (4%)
  other arithmetic  3.41 us (3%)
    all_gather x1, waiting for transfers between devices, shards(): keys = lax.all_gather(packed, 'ctx', axis=0, tiled=False)  47.8 us
    pallas_call x1, Pallas kernels, compute(): pl.pallas_call(compute_kernel, grid_spec=spec, out_shape=[jax.ShapeDtypeS...  27.9 us
    all_to_all x1, blocking collectives, shards(): lax.all_to_all(outgoing, 'ctx', split_axis=0, concat_axis=0, tiled=True)  27.7 us
    unnamed x8, local copies, waits for them, and re-layouts  4.78 us
  transfers between devices with their start and end apart: 1, of which 1 were waited for; matrix products, arithmetic and copies ran while one was open for 1% of the time, Pallas kernels for 0%

profile of v1, /device:TPU:0, one launch (start us, length us, event | category | flops | bytes accessed | tf_op | source)
XLA Modules:
  0.0 125.7 jit_solution(12704456210051860986)
XLA Ops:
  7.2 0.0 all-gather.3.cloned.1.call-start
  7.2 1.6 %pad_maximum_fusion = bf16[704,128]{1,0:T(8,128)(2,1)} fusion(bf16[128,128]{1,0:T(8,128)(2,1)} %param.9, bf16[576,128]{1,0:T(8,128)(2,1)} %param.7), kind=kLoop, calls=%fused_computation.1 | loop fusion | flops 360448 | bytes 360448 | tf_op jit(solution)/shard_map/concatenate | solution.py:162
  8.8 0.0 all-gather.3.cloned.1.call-update
  8.9 0.7 iota_compare_fusion
  9.6 47.8 %all-gather.3.cloned.1.call-done = bf16[11264,128]{1,0:T(8,128)(2,1)} async-done(((bf16[704,128]{1,0:T(8,128)(2,1)}), bf16[11264,128]{1,0:T(8,128)(2,1)}) %all-gather.3.cloned.1.call-update) | async-done | bytes 2883600 | tf_op jit(solution)/shard_map/all_gather | solution.py:163
  57.4 0.0 copy-start
  57.4 1.8 %copy-done = bf16[11264,128]{1,0:T(8,128)(2,1)S(1)} copy-done((bf16[11264,128]{1,0:T(8,128)(2,1)S(1)}, bf16[11264,128]{1,0:T(8,128)(2,1)}, u32[]{:S(2)}) %copy-start) | copy-done | bytes 2883608
  59.2 0.0 copy-start.1
  59.2 1.6 %copy-done.1 = bf16[64,128,128]{2,1,0:T(8,128)(2,1)S(1)} copy-done((bf16[64,128,128]{2,1,0:T(8,128)(2,1)S(1)}, bf16[64,128,128]{2,1,0:T(8,128)(2,1)}, u32[]{:S(2)}) %copy-start.1) | copy-done | bytes 2097176
  60.8 0.0 copy-start.2
  60.8 0.7 copy-done.2
  61.5 0.0 copy-start.3
  61.5 0.7 copy-done.3
  62.2 27.9 %shard_map.85 = (f32[1,128]{1,0:T(1,128)}, f32[64,128]{1,0:T(8,128)}, f32[4,128,128]{2,1,0:T(8,128)S(1)}) custom-call(s32[1,4]{1,0:T(1,128)S(1)} %copy-done.3, bf16[64,576,128]{2,1,0:T(8,128)(2,1)} %mq.1, bf16[64,128,128]{2,1,0:T(8,128)(2,1)S(1)} %copy-done.1, bf16[64,128]{1,0:T(8,128)(2,1)S(1)} %copy-done.2, bf16[16,704,128]{2,1,0:T(8,128)(2,1)S(1)} %bitcast.19, ...), custom_call_target="tpu_custom_call" | custom-call | tf_op jit(solution)/shard_map/pallas_call | solution.py:146
  90.1 0.4 select_add_fusion
  90.5 27.7 %all_to_all.5 = f32[16,128,128]{2,1,0:T(8,128)S(1)} all-to-all(f32[16,128,128]{2,1,0:T(8,128)S(1)} %select_add_fusion), channel_id=1, replica_groups=mesh['groups'=2,'ctx'=16] {'ctx'}, dimensions={0} | all-to-all | bytes 2097152 | tf_op jit(solution)/shard_map/all_to_all | solution.py:172
  118.1 0.7 reduce_sum.9
  (2 shorter events, 0.0 us)
Async XLA Ops:
  7.2 50.2 %all-gather.3.cloned.1.call-start = ((), (), s32[]{:S(2)}) async-start(), calls=%async_computation.1 | async-start | bytes 3063808 | tf_op jit(solution)/shard_map/all_gather | solution.py:163
  57.4 1.8 %copy-start = (bf16[11264,128]{1,0:T(8,128)(2,1)S(1)}, bf16[11264,128]{1,0:T(8,128)(2,1)}, u32[]{:S(2)}) copy-start(bf16[11264,128]{1,0:T(8,128)(2,1)} %all-gather.3.cloned.1.call-done) | copy-start | bytes 8650756
  59.2 1.6 %copy-start.1 = (bf16[64,128,128]{2,1,0:T(8,128)(2,1)S(1)}, bf16[64,128,128]{2,1,0:T(8,128)(2,1)}, u32[]{:S(2)}) copy-start(bf16[64,128,128]{2,1,0:T(8,128)(2,1)} %iq.1) | copy-start | bytes 6291460
  60.8 0.7 copy-start.2
  61.5 0.7 copy-start.3
Sparse Core Ops, SparseCore 0:
  10.3 47.0 all-gather.2

commit v2 on v1

--- a/solution.py
+++ b/solution.py
@@ -155,22 +155,277 @@
     )(picks, mq, iq, hw, keys, keys, keys, keys)
 
 
+mesh_ids = pl.DeviceIdType.MESH
+
+
+def layout(count):
+    half = count // 2
+    mid = 1
+    while 4 * mid * mid <= half:
+        mid *= 2
+    return half // mid, mid
+
+
+def position(mid):
+    me = lax.axis_index("ctx")
+    return me // (2 * mid), lax.rem(me // 2, mid), lax.rem(me, 2)
+
+
+def greet(peers):
+    barrier = pltpu.get_barrier_semaphore()
+    for peer in peers:
+        pl.semaphore_signal(barrier, inc=1, device_id={"ctx": peer}, device_id_type=mesh_ids)
+    pl.semaphore_wait(barrier, len(peers))
+
+
+def gather_kernel(count, main_ref, index_ref, out, local_sem, recv, zsend, ysend, csend):
+    outer, mid = layout(count)
+    a, y, c = position(mid)
+    latent = main_ref.shape[0]
+    channels = latent + index_ref.shape[0]
+
+    def name(level, row, core):
+        return (level * mid + row) * 2 + core
+
+    me = name(a, y, c)
+    own = [
+        pltpu.make_async_copy(main_ref, out.at[me, pl.ds(0, latent)], local_sem.at[0]),
+        pltpu.make_async_copy(
+            index_ref, out.at[me, pl.ds(latent, channels - latent)], local_sem.at[1]
+        ),
+    ]
+    for copy in own:
+        copy.start()
+    greet(
+        [name(lax.rem(a + d, outer), y, c) for d in range(1, outer)]
+        + [name(a, lax.rem(y + d, mid), c) for d in range(1, mid)]
+        + [name(a, y, 1 - c)]
+    )
+    for copy in own:
+        copy.wait()
+
+    def send(block, peer, sem):
+        return pltpu.make_async_remote_copy(
+            src_ref=out.at[block],
+            dst_ref=out.at[block],
+            send_sem=sem,
+            recv_sem=recv.at[block],
+            device_id={"ctx": peer},
+            device_id_type=mesh_ids,
+        )
+
+    def up(k):
+        return send(name(a - k, y, c), name(a + 1, y, c), zsend.at[k])
+
+    def side(k, d):
+        return send(
+            name(a - k, y, c), name(a, lax.rem(y + d, mid), c), ysend.at[k * max(mid - 1, 1) + d - 1]
+        )
+
+    def across(k, d):
+        return send(
+            name(a - k, lax.rem(y + d, mid), c), name(a, y, 1 - c), csend.at[k * mid + d]
+        )
+
+    def arrive(block):
+        send(block, name(a, y, 1 - c), csend.at[0]).wait_recv()
+
+    def first(k):
+        @pl.when(a >= k)
+        def _():
+            if k > 0:
+                arrive(name(a - k, y, c))
+
+            @pl.when(a + 1 < outer)
+            def _():
+                up(k).start()
+
+            for d in range(1, mid):
+                side(k, d).start()
+            across(k, 0).start()
+
+    def second(k):
+        @pl.when(a >= k)
+        def _():
+            for d in range(1, mid):
+                arrive(name(a - k, lax.rem(y + d, mid), c))
+                across(k, d).start()
+
+    for k in range(outer):
+        first(k)
+        if k > 0:
+            second(k - 1)
+    second(outer - 1)
+    for k in range(outer):
+
+        @pl.when(a >= k)
+        def _():
+            for d in range(mid):
+                arrive(name(a - k, lax.rem(y + d, mid), 1 - c))
+
+            @pl.when(a + 1 < outer)
+            def _():
+                up(k).wait_send()
+
+            for d in range(1, mid):
+                side(k, d).wait_send()
+            for d in range(mid):
+                across(k, d).wait_send()
+
+
+def gather(main_keys, index_keys):
+    count = lax.axis_size("ctx")
+    outer, mid = layout(count)
+    channels = main_keys.shape[0] + index_keys.shape[0]
+    return pl.pallas_call(
+        functools.partial(gather_kernel, count),
+        out_shape=jax.ShapeDtypeStruct((count, channels, main_keys.shape[1]), jnp.bfloat16),
+        in_specs=[pl.BlockSpec(memory_space=pl.ANY)] * 2,
+        out_specs=pl.BlockSpec(memory_space=pl.ANY),
+        scratch_shapes=[
+            pltpu.SemaphoreType.DMA((2,)),
+            pltpu.SemaphoreType.DMA((count,)),
+            pltpu.SemaphoreType.DMA((outer,)),
+            pltpu.SemaphoreType.DMA((outer * max(mid - 1, 1),)),
+            pltpu.SemaphoreType.DMA((outer * mid,)),
+        ],
+        compiler_params=pltpu.CompilerParams(collective_id=0, has_side_effects=True),
+    )(main_keys, index_keys)
+
+
+def scatter_kernel(count, terms, out, buf1, sum1, buf2, sum2, buf3, s1, r1, s2, r2, s3, r3):
+    outer, mid = layout(count)
+    a, y, c = position(mid)
+    others = max(mid - 1, 1)
+
+    def name(level, row, core):
+        return (level * mid + row) * 2 + core
+
+    greet(
+        [name(lax.rem(a + d, outer), y, c) for d in range(1, outer)]
+        + [name(a, lax.rem(y + d, mid), c) for d in range(1, mid)]
+        + [name(a, y, 1 - c)]
+    )
+
+    def send(src, dst, send_sem, recv_sem, peer):
+        return pltpu.make_async_remote_copy(
+            src_ref=src,
+            dst_ref=dst,
+            send_sem=send_sem,
+            recv_sem=recv_sem,
+            device_id={"ctx": peer},
+            device_id_type=mesh_ids,
+        )
+
+    def across(k):
+        return send(terms.at[1 - c, k], buf1.at[k], s1.at[k], r1.at[k], name(a, y, 1 - c))
+
+    def side(k, d):
+        row = lax.rem(y + d, mid)
+        spot = k * others + d - 1
+        return send(sum1.at[k, row], buf2.at[spot], s2.at[spot], r2.at[spot], name(a, row, c))
+
+    def down(k):
+        spot = a - k - 1
+        return send(sum2.at[k], buf3.at[spot], s3.at[k], r3.at[spot], name(k, y, c))
+
+    for k in range(outer):
+
+        @pl.when(a >= k)
+        def _():
+            across(k).start()
+
+    for k in range(outer):
+
+        @pl.when(a >= k)
+        def _():
+            across(k).wait_recv()
+            sum1[k] = terms[c, k] + buf1[k]
+            for d in range(1, mid):
+                side(k, d).start()
+
+    for k in range(outer):
+
+        @pl.when(a >= k)
+        def _():
+            total = sum1[k, y]
+            for d in range(1, mid):
+                side(k, d).wait_recv()
+                total = total + buf2[k * others + d - 1]
+            sum2[k] = total
+
+            @pl.when(a > k)
+            def _():
+                down(k).start()
+
+            @pl.when(a == k)
+            def _():
+                out[...] = total
+
+    for d in range(outer - 1):
+
+        @pl.when(a + d + 1 < outer)
+        def _():
+            send(sum2.at[0], buf3.at[d], s3.at[0], r3.at[d], name(a, y, 1 - c)).wait_recv()
+            out[...] += buf3[d]
+
+    for k in range(outer):
+
+        @pl.when(a >= k)
+        def _():
+            across(k).wait_send()
+            for d in range(1, mid):
+                side(k, d).wait_send()
+
+            @pl.when(a > k)
+            def _():
+                down(k).wait_send()
+
+
+def scatter(terms):
+    count = lax.axis_size("ctx")
+    outer, mid = layout(count)
+    others = max(mid - 1, 1)
+    tile = terms.shape[3:]
+    return pl.pallas_call(
+        functools.partial(scatter_kernel, count),
+        out_shape=jax.ShapeDtypeStruct(tile, jnp.float32),
+        in_specs=[pl.BlockSpec(memory_space=pltpu.VMEM)],
+        out_specs=pl.BlockSpec(memory_space=pltpu.VMEM),
+        scratch_shapes=[
+            pltpu.VMEM((outer, mid) + tile, jnp.float32),
+            pltpu.VMEM((outer, mid) + tile, jnp.float32),
+            pltpu.VMEM((outer * others,) + tile, jnp.float32),
+            pltpu.VMEM((outer,) + tile, jnp.float32),
+            pltpu.VMEM((outer - 1,) + tile, jnp.float32),
+            pltpu.SemaphoreType.DMA((outer,)),
+            pltpu.SemaphoreType.DMA((outer,)),
+            pltpu.SemaphoreType.DMA((outer * others,)),
+            pltpu.SemaphoreType.DMA((outer * others,)),
+            pltpu.SemaphoreType.DMA((outer,)),
+            pltpu.SemaphoreType.DMA((outer - 1,)),
+        ],
+        compiler_params=pltpu.CompilerParams(
+            collective_id=1, has_side_effects=True, vmem_limit_bytes=48 * 1024 * 1024
+        ),
+    )(terms)
+
+
 def shards(main_queries, main_keys, index_queries, index_keys, head_weights, block_picks):
     tok = main_queries.shape[2]
     picks = block_picks
     count = lax.axis_size("ctx")
-    packed = jnp.concatenate([main_keys, index_keys], axis=0)
-    keys = lax.all_gather(packed, "ctx", axis=0, tiled=False)
+    keys = gather(main_keys, index_keys)
     row_loss, weight_grad, slot_grads = compute(
         picks, main_queries, index_queries, head_weights, keys
     )
-    owners = jnp.arange(count, dtype=jnp.int32)
-    match = picks[0][:, None] == owners[None, :]
-    outgoing = jnp.zeros((count,) + slot_grads.shape[1:], jnp.float32)
+    outer, mid = layout(count)
+    owners = jnp.arange(count, dtype=jnp.int32).reshape(outer, mid, 2).transpose(2, 0, 1)
+    terms = jnp.zeros(owners.shape + slot_grads.shape[1:], jnp.float32)
     for slot in range(4):
-        outgoing = outgoing + jnp.where(match[slot][:, None, None], slot_grads[slot][None], 0.0)
-    arrived = lax.all_to_all(outgoing, "ctx", split_axis=0, concat_axis=0, tiled=True)
-    key_grad = jnp.sum(arrived, axis=0)
+        match = (picks[0, slot] == owners)[..., None, None]
+        terms = terms + jnp.where(match, slot_grads[slot], 0.0)
+    key_grad = scatter(terms)
     return (row_loss.reshape(tok), weight_grad, key_grad)
 
 

time: 126 us -> 78.8 us (0.63)
  waiting for transfers between devices: 47.8 us -> 0 us
  Pallas kernels: 27.9 us -> 71.8 us
  blocking collectives: 27.7 us -> 0 us
  between operations: 14 us -> 0.73 us
  local copies, waits for them, and re-layouts: 4.81 us -> 3.12 us
    all_gather x1 -> x0, waiting for transfers between devices: 47.8 us -> none  [shards(): keys = lax.all_gather(packed, 'ctx', axis=0, tiled=False)]
    pallas_call x0 -> x2, Pallas kernels: none -> 43.9 us  [the longest x1 27.8 us: scatter(): pl.pallas_call(functools.partial(scatter_kernel, count), out_shape=jax.Sh...]
    all_to_all x1 -> x0, blocking collectives: 27.7 us -> none  [shards(): lax.all_to_all(outgoing, 'ctx', split_axis=0, concat_axis=0, tiled=True)]
    unnamed x8 -> x9, local copies, waits for them, and re-layouts: 4.78 us -> 2.45 us
    eq x1 -> x2, other arithmetic: 0.73 us -> 2.6 us  [shards(): match = (picks[0, slot] == owners)[..., None, None]]
    concatenate x1 -> x0, other arithmetic: 1.62 us -> none  [shards(): packed = jnp.concatenate([main_keys, index_keys], axis=0)]
  transfers between devices with their start and end apart: 1 -> 0, of which waited for: 1 -> 0; matrix products, arithmetic and copies ran while one was open for 1% -> 0% of each run, Pallas kernels for 0% -> 0%
where the time goes in v2:
time: 78.8 us; the launch traced here: 78.6 us
  Pallas kernels  71.8 us (91%)
  local copies, waits for them, and re-layouts  3.12 us (4%)
  other arithmetic  2.97 us (4%)
    pallas_call x1, Pallas kernels, compute(): pl.pallas_call(compute_kernel, grid_spec=spec, out_shape=[jax.ShapeDtypeS...  27.8 us
    pallas_call x1, Pallas kernels, scatter(): pl.pallas_call(functools.partial(scatter_kernel, count), out_shape=jax.Sh...  27.8 us
    pallas_call x1, Pallas kernels, gather(): pl.pallas_call(functools.partial(gather_kernel, count), out_shape=jax.Sha...  16.2 us
    eq x2, other arithmetic, shards(): match = (picks[0, slot] == owners)[..., None, None]  2.6 us
    unnamed x9, local copies, waits for them, and re-layouts  2.45 us

profile of v2, /device:TPU:0, one launch (start us, length us, event | category | flops | bytes accessed | tf_op | source)
XLA Modules:
  0.0 78.6 jit_solution(1197899688278037622)
XLA Ops:
  0.6 0.0 copy-start.3
  0.6 0.0 copy-start.1
  0.7 0.0 copy-start.2
  0.7 16.2 %shard_map.85.k0.k1.k2.k3 = bf16[16,704,128]{2,1,0:T(8,128)(2,1)} custom-call(bf16[576,128]{1,0:T(8,128)(2,1)} %main_ref.1, bf16[128,128]{1,0:T(8,128)(2,1)} %index_ref.1), custom_call_target="tpu_custom_call" | custom-call | tf_op jit(solution)/shard_map/pallas_call | solution.py:280
  16.8 0.0 copy-done.3
  16.8 0.0 copy-done.1
  16.8 0.0 copy-done.2
  16.9 0.0 copy-start
  16.9 1.8 %copy-done = bf16[16,704,128]{2,1,0:T(8,128)(2,1)S(1)} copy-done((bf16[16,704,128]{2,1,0:T(8,128)(2,1)S(1)}, bf16[16,704,128]{2,1,0:T(8,128)(2,1)}, u32[]{:S(2)}) %copy-start) | copy-done | bytes 2883608
  18.7 27.8 %shard_map.86 = (f32[1,128]{1,0:T(1,128)}, f32[64,128]{1,0:T(8,128)}, f32[4,128,128]{2,1,0:T(8,128)S(1)}) custom-call(s32[1,4]{1,0:T(1,128)S(1)} %copy-done.3, bf16[64,576,128]{2,1,0:T(8,128)(2,1)} %mq.1, bf16[64,128,128]{2,1,0:T(8,128)(2,1)S(1)} %copy-done.1, bf16[64,128]{1,0:T(8,128)(2,1)S(1)} %copy-done.2, bf16[16,704,128]{2,1,0:T(8,128)(2,1)S(1)} %copy-done, ...), custom_call_target="tpu_custom_call" | custom-call | tf_op jit(solution)/shard_map/pallas_call | solution.py:146
  46.5 0.7 fusion.4
  47.2 1.3 %fusion = (pred[2,4,2]{2,1,0:T(4,128)(4,1)S(1)}, pred[2,4,2]{2,1,0:T(4,128)(4,1)S(1)}) fusion(s32[]{:T(128)} %bitcast.7, s32[]{:T(128)} %bitcast.5), kind=kLoop, calls=%fused_computation.6 | loop fusion | flops 96 | bytes 40 | tf_op jit(solution)/shard_map/eq | solution.py:426
  48.5 1.3 %fusion.2 = (pred[2,4,2]{2,1,0:T(4,128)(4,1)S(1)}, pred[2,4,2]{2,1,0:T(4,128)(4,1)S(1)}) fusion(s32[]{:T(128)} %bitcast.3, s32[]{:T(128)} %bitcast.1), kind=kLoop, calls=%fused_computation.8 | loop fusion | flops 96 | bytes 40 | tf_op jit(solution)/shard_map/eq | solution.py:426
  49.8 0.4 select_add_fusion.terms
  50.2 27.8 %shard_map.87 = f32[128,128]{1,0:T(8,128)S(1)} custom-call(f32[2,4,2,128,128]{4,3,2,1,0:T(8,128)S(1)} %select_add_fusion.terms), custom_call_target="tpu_custom_call" | custom-call | tf_op jit(solution)/shard_map/pallas_call | solution.py:390
  78.0 0.6 copy.10
  (1 shorter events, 0.0 us)
Async XLA Ops:
  0.6 16.2 %copy-start.3 = (s32[1,4]{1,0:T(1,128)S(1)}, s32[1,4]{1,0:T(1,128)}, u32[]{:S(2)}) copy-start(s32[1,4]{1,0:T(1,128)} %picks.1) | copy-start | bytes 52
  0.6 16.2 %copy-start.1 = (bf16[64,128,128]{2,1,0:T(8,128)(2,1)S(1)}, bf16[64,128,128]{2,1,0:T(8,128)(2,1)}, u32[]{:S(2)}) copy-start(bf16[64,128,128]{2,1,0:T(8,128)(2,1)} %iq.1) | copy-start | bytes 6291460
  0.7 16.2 %copy-start.2 = (bf16[64,128]{1,0:T(8,128)(2,1)S(1)}, bf16[64,128]{1,0:T(8,128)(2,1)}, u32[]{:S(2)}) copy-start(bf16[64,128]{1,0:T(8,128)(2,1)} %hw.1) | copy-start | bytes 49156
  16.9 1.8 %copy-start = (bf16[16,704,128]{2,1,0:T(8,128)(2,1)S(1)}, bf16[16,704,128]{2,1,0:T(8,128)(2,1)}, u32[]{:S(2)}) copy-start(bf16[16,704,128]{2,1,0:T(8,128)(2,1)} %shard_map.85.k0.k1.k2.k3) | copy-start | bytes 8650756

commit v3 on v2

--- a/solution.py
+++ b/solution.py
@@ -43,6 +43,7 @@
         wf[...] = hw[...].astype(jnp.float32)
         acc[...] = jnp.zeros_like(acc)
         raw[...] = jnp.zeros_like(raw)
+        slot_ref[...] = jnp.zeros_like(slot_ref)
 
     scale2 = main_scale * log2e
 
@@ -103,7 +104,13 @@
 
         lax.fori_loop(0, index_heads // 2, back_pair, 0, unroll=2)
         for slot in range(slots):
-            slot_ref[slot] = (kt[pl.ds(slot * tok, tok), :] * index_scale).T
+            part = (kt[pl.ds(slot * tok, tok), :] * index_scale).T
+            owner = picks[0, slot]
+            half = slot_ref.shape[0] // 2
+
+            @pl.when(owner >= 0)
+            def _():
+                slot_ref[lax.rem(owner, 2) * half + owner // 2] = part
 
 
 def compute(picks, mq, iq, hw, keys):
@@ -111,6 +118,7 @@
     index_heads, dim, _ = iq.shape
     channels = latent + dim
     group = 8
+    count = keys.shape[0]
     width = 4 * tok
 
     def key_spec(slot):
@@ -130,7 +138,7 @@
         out_specs=[
             pl.BlockSpec((1, tok), lambda g, p: (0, 0)),
             pl.BlockSpec((index_heads, tok), lambda g, p: (0, 0)),
-            pl.BlockSpec((4, dim, tok), lambda g, p: (0, 0, 0)),
+            pl.BlockSpec((count, dim, tok), lambda g, p: (0, 0, 0)),
         ],
         scratch_shapes=[
             pltpu.VMEM((width, latent + tok), jnp.bfloat16),
@@ -149,7 +157,7 @@
         out_shape=[
             jax.ShapeDtypeStruct((1, tok), jnp.float32),
             jax.ShapeDtypeStruct((index_heads, tok), jnp.float32),
-            jax.ShapeDtypeStruct((4, dim, tok), jnp.float32),
+            jax.ShapeDtypeStruct((count, dim, tok), jnp.float32),
         ],
         compiler_params=pltpu.CompilerParams(vmem_limit_bytes=48 * 1024 * 1024),
     )(picks, mq, iq, hw, keys, keys, keys, keys)
@@ -416,15 +424,11 @@
     picks = block_picks
     count = lax.axis_size("ctx")
     keys = gather(main_keys, index_keys)
-    row_loss, weight_grad, slot_grads = compute(
+    row_loss, weight_grad, placed = compute(
         picks, main_queries, index_queries, head_weights, keys
     )
     outer, mid = layout(count)
-    owners = jnp.arange(count, dtype=jnp.int32).reshape(outer, mid, 2).transpose(2, 0, 1)
-    terms = jnp.zeros(owners.shape + slot_grads.shape[1:], jnp.float32)
-    for slot in range(4):
-        match = (picks[0, slot] == owners)[..., None, None]
-        terms = terms + jnp.where(match, slot_grads[slot], 0.0)
+    terms = placed.reshape((2, outer, mid) + placed.shape[1:])
     key_grad = scatter(terms)
     return (row_loss.reshape(tok), weight_grad, key_grad)
 

time: 78.8 us -> 75.4 us (0.957)
  other arithmetic: 2.97 us -> 0 us
    eq x2 -> x0, other arithmetic: 2.6 us -> none  [shards(): match = (picks[0, slot] == owners)[..., None, None]]
where the time goes in v3:
time: 75.4 us; the launch traced here: 75.2 us
  Pallas kernels  72 us (95%)
  local copies, waits for them, and re-layouts  2.45 us (3%)
    pallas_call x1, Pallas kernels, compute(): pl.pallas_call(compute_kernel, grid_spec=spec, out_shape=[jax.ShapeDtypeS...  28.2 us
    pallas_call x1, Pallas kernels, scatter(): pl.pallas_call(functools.partial(scatter_kernel, count), out_shape=jax.Sh...  27.7 us
    pallas_call x1, Pallas kernels, gather(): pl.pallas_call(functools.partial(gather_kernel, count), out_shape=jax.Sha...  16.2 us
    unnamed x9, local copies, waits for them, and re-layouts  2.45 us

profile of v3, /device:TPU:0, one launch (start us, length us, event | category | flops | bytes accessed | tf_op | source)
XLA Modules:
  0.0 75.2 jit_solution(3320686467957820610)
XLA Ops:
  0.6 0.0 copy-start.3
  0.6 0.0 copy-start.2
  0.7 0.0 copy-start.1
  0.7 16.2 %shard_map.85.k0.k1.k2.k3 = bf16[16,704,128]{2,1,0:T(8,128)(2,1)} custom-call(bf16[576,128]{1,0:T(8,128)(2,1)} %main_ref.1, bf16[128,128]{1,0:T(8,128)(2,1)} %index_ref.1), custom_call_target="tpu_custom_call" | custom-call | tf_op jit(solution)/shard_map/pallas_call | solution.py:288
  16.8 0.0 copy-done.3
  16.8 0.0 copy-done.2
  16.8 0.0 copy-done.1
  16.9 0.0 copy-start
  16.9 1.8 %copy-done = bf16[16,704,128]{2,1,0:T(8,128)(2,1)S(1)} copy-done((bf16[16,704,128]{2,1,0:T(8,128)(2,1)S(1)}, bf16[16,704,128]{2,1,0:T(8,128)(2,1)}, u32[]{:S(2)}) %copy-start) | copy-done | bytes 2883608
  18.7 28.2 %shard_map.86 = (f32[1,128]{1,0:T(1,128)}, f32[64,128]{1,0:T(8,128)}, f32[16,128,128]{2,1,0:T(8,128)S(1)}) custom-call(s32[1,4]{1,0:T(1,128)S(1)} %copy-done.3, bf16[64,576,128]{2,1,0:T(8,128)(2,1)} %mq.1, bf16[64,128,128]{2,1,0:T(8,128)(2,1)S(1)} %copy-done.1, bf16[64,128]{1,0:T(8,128)(2,1)S(1)} %copy-done.2, bf16[16,704,128]{2,1,0:T(8,128)(2,1)S(1)} %copy-done, ...), custom_call_target="tpu_custom_call" | custom-call | tf_op jit(solution)/shard_map/pallas_call | solution.py:154
  46.9 27.7 %shard_map.87 = f32[128,128]{1,0:T(8,128)S(1)} custom-call(f32[2,4,2,128,128]{4,3,2,1,0:T(8,128)S(1)} %bitcast.2), custom_call_target="tpu_custom_call" | custom-call | tf_op jit(solution)/shard_map/pallas_call | solution.py:398
  74.6 0.6 copy.10
Async XLA Ops:
  0.6 16.2 %copy-start.3 = (s32[1,4]{1,0:T(1,128)S(1)}, s32[1,4]{1,0:T(1,128)}, u32[]{:S(2)}) copy-start(s32[1,4]{1,0:T(1,128)} %picks.1) | copy-start | bytes 52
  0.6 16.2 %copy-start.2 = (bf16[64,128]{1,0:T(8,128)(2,1)S(1)}, bf16[64,128]{1,0:T(8,128)(2,1)}, u32[]{:S(2)}) copy-start(bf16[64,128]{1,0:T(8,128)(2,1)} %hw.1) | copy-start | bytes 49156
  0.7 16.2 %copy-start.1 = (bf16[64,128,128]{2,1,0:T(8,128)(2,1)S(1)}, bf16[64,128,128]{2,1,0:T(8,128)(2,1)}, u32[]{:S(2)}) copy-start(bf16[64,128,128]{2,1,0:T(8,128)(2,1)} %iq.1) | copy-start | bytes 6291460
  16.9 1.8 %copy-start = (bf16[16,704,128]{2,1,0:T(8,128)(2,1)S(1)}, bf16[16,704,128]{2,1,0:T(8,128)(2,1)}, u32[]{:S(2)}) copy-start(bf16[16,704,128]{2,1,0:T(8,128)(2,1)} %shard_map.85.k0.k1.k2.k3) | copy-start | bytes 8650756

commit v4 on v3

--- a/solution.py
+++ b/solution.py
@@ -66,7 +66,7 @@
         raw[...] += a[:, :tok] + a[:, tok:]
         return 0
 
-    lax.fori_loop(0, heads // 2, main_pair, 0, unroll=2)
+    lax.fori_loop(0, heads // 2, main_pair, 0, unroll=4)
 
     @pl.when(step == steps - 1)
     def _():
@@ -102,7 +102,7 @@
             )
             return 0
 
-        lax.fori_loop(0, index_heads // 2, back_pair, 0, unroll=2)
+        lax.fori_loop(0, index_heads // 2, back_pair, 0, unroll=4)
         for slot in range(slots):
             part = (kt[pl.ds(slot * tok, tok), :] * index_scale).T
             owner = picks[0, slot]

time: 75.4 us -> 71.7 us (0.951)
  Pallas kernels: 72 us -> 68.3 us
    pallas_call x1, Pallas kernels: 28.2 us -> 24.5 us  [compute(): pl.pallas_call(compute_kernel, grid_spec=spec, out_shape=[jax.ShapeDtypeS...]
where the time goes in v4:
time: 71.7 us; the launch traced here: 71.5 us
  Pallas kernels  68.3 us (95%)
  local copies, waits for them, and re-layouts  2.45 us (3%)
    pallas_call x1, Pallas kernels, scatter(): pl.pallas_call(functools.partial(scatter_kernel, count), out_shape=jax.Sh...  27.7 us
    pallas_call x1, Pallas kernels, compute(): pl.pallas_call(compute_kernel, grid_spec=spec, out_shape=[jax.ShapeDtypeS...  24.5 us
    pallas_call x1, Pallas kernels, gather(): pl.pallas_call(functools.partial(gather_kernel, count), out_shape=jax.Sha...  16.2 us
    unnamed x9, local copies, waits for them, and re-layouts  2.45 us

profile of v4, /device:TPU:0, one launch (start us, length us, event | category | flops | bytes accessed | tf_op | source)
XLA Modules:
  0.0 71.5 jit_solution(17044216628458598744)
XLA Ops:
  0.6 0.0 copy-start.3
  0.6 0.0 copy-start.2
  0.7 0.0 copy-start.1
  0.7 16.2 %shard_map.85.k0.k1.k2.k3 = bf16[16,704,128]{2,1,0:T(8,128)(2,1)} custom-call(bf16[576,128]{1,0:T(8,128)(2,1)} %main_ref.1, bf16[128,128]{1,0:T(8,128)(2,1)} %index_ref.1), custom_call_target="tpu_custom_call" | custom-call | tf_op jit(solution)/shard_map/pallas_call | solution.py:288
  16.8 0.0 copy-done.3
  16.8 0.0 copy-done.2
  16.8 0.0 copy-done.1
  16.9 0.0 copy-start
  16.9 1.8 %copy-done = bf16[16,704,128]{2,1,0:T(8,128)(2,1)S(1)} copy-done((bf16[16,704,128]{2,1,0:T(8,128)(2,1)S(1)}, bf16[16,704,128]{2,1,0:T(8,128)(2,1)}, u32[]{:S(2)}) %copy-start) | copy-done | bytes 2883608
  18.7 24.5 %shard_map.86 = (f32[1,128]{1,0:T(1,128)}, f32[64,128]{1,0:T(8,128)}, f32[16,128,128]{2,1,0:T(8,128)S(1)}) custom-call(s32[1,4]{1,0:T(1,128)S(1)} %copy-done.3, bf16[64,576,128]{2,1,0:T(8,128)(2,1)} %mq.1, bf16[64,128,128]{2,1,0:T(8,128)(2,1)S(1)} %copy-done.1, bf16[64,128]{1,0:T(8,128)(2,1)S(1)} %copy-done.2, bf16[16,704,128]{2,1,0:T(8,128)(2,1)S(1)} %copy-done, ...), custom_call_target="tpu_custom_call" | custom-call | tf_op jit(solution)/shard_map/pallas_call | solution.py:154
  43.1 27.7 %shard_map.87 = f32[128,128]{1,0:T(8,128)S(1)} custom-call(f32[2,4,2,128,128]{4,3,2,1,0:T(8,128)S(1)} %bitcast.2), custom_call_target="tpu_custom_call" | custom-call | tf_op jit(solution)/shard_map/pallas_call | solution.py:398
  70.9 0.6 copy.10
Async XLA Ops:
  0.6 16.2 %copy-start.3 = (s32[1,4]{1,0:T(1,128)S(1)}, s32[1,4]{1,0:T(1,128)}, u32[]{:S(2)}) copy-start(s32[1,4]{1,0:T(1,128)} %picks.1) | copy-start | bytes 52
  0.6 16.2 %copy-start.2 = (bf16[64,128]{1,0:T(8,128)(2,1)S(1)}, bf16[64,128]{1,0:T(8,128)(2,1)}, u32[]{:S(2)}) copy-start(bf16[64,128]{1,0:T(8,128)(2,1)} %hw.1) | copy-start | bytes 49156
  0.7 16.2 %copy-start.1 = (bf16[64,128,128]{2,1,0:T(8,128)(2,1)S(1)}, bf16[64,128,128]{2,1,0:T(8,128)(2,1)}, u32[]{:S(2)}) copy-start(bf16[64,128,128]{2,1,0:T(8,128)(2,1)} %iq.1) | copy-start | bytes 6291460
  16.9 1.8 %copy-start = (bf16[16,704,128]{2,1,0:T(8,128)(2,1)S(1)}, bf16[16,704,128]{2,1,0:T(8,128)(2,1)}, u32[]{:S(2)}) copy-start(bf16[16,704,128]{2,1,0:T(8,128)(2,1)} %shard_map.85.k0.k1.k2.k3) | copy-start | bytes 8650756
